TPU v7x, 32 devices: a whole 2x2x4 slice. The times are simulated.
32 devices in a mesh: group: 2 (over x), expert: 16 (over z, y, core).
Axes of the slice: x: 2, y: 2, z: 4, core: 2. Of those that a mesh axis runs over, the one named last changes fastest.
Arguments:
- tokens: bfloat16 [128, 7168], P(('group', 'expert')), parts along dimension 0, may hold values from -6 to 6
- expert_ids: int32 [128, 2], P(('group', 'expert')), parts along dimension 0, may hold values from 0 to 1, all different within a row; in each aligned block of 4 rows (0 to 3, 4 to 7, ...) at most 4 rows name the same one
- gate_codes: int32 [128, 2], P(('group', 'expert')), parts along dimension 0, may hold values from 1 to 65535
- gate_weight: bfloat16 [16, 7168, 256], P('expert'), may hold values from -0.0625 to 0.0625
- up_weight: bfloat16 [16, 7168, 256], P('expert'), may hold values from -0.0625 to 0.0625
- down_weight: bfloat16 [16, 256, 7168], P('expert'), may hold values from -0.125 to 0.125
- target_basis: bfloat16 [7168, 512], P('expert'), may hold values from -0.0625 to 0.0625
Outputs:
- targets: bfloat16 [128, 512], P(('group', 'expert')), parts along dimension 0
There are 2 independent parts, one for each index of `group`. A program takes and returns all parts, laid end to end along the dimension named above; an argument that names none is the same for every part. Nothing has to cross between parts.
Inputs may be any that keep to these rules, and one draw needn't show every extreme that they name: `expert_ids`: each row names 2 different experts; among the 4 rows of one device no expert is named more than 4 times, a bound that some block reaches.
All inputs are finite; a program needn't handle non-finite values.
Results may differ from a plain program's by a relative error of at most 0.0057.
Values may be sent and summed in bfloat16 or wider, within the bound.
A program may use at most 128 MiB of HBM per device.

v0:
```python
import jax
import jax.numpy as jnp
from jax import lax
from jax.sharding import PartitionSpec as P

SLICES = 8


def run_expert(received, gate_weight, up_weight, down_weight):
    sources, slots, feature_width = received.shape
    row_block = received.reshape(sources * slots, feature_width)
    gate_act = jnp.dot(row_block, gate_weight[0], preferred_element_type=jnp.float32)
    up_act = jnp.dot(row_block, up_weight[0], preferred_element_type=jnp.float32)
    hidden = (jax.nn.silu(gate_act) * up_act).astype(jnp.bfloat16)
    expert_part = jnp.dot(hidden, down_weight[0], preferred_element_type=jnp.float32).astype(
        jnp.bfloat16
    )
    return expert_part.reshape(sources, slots, feature_width)


def shards(tokens, expert_ids, gate_codes, gate_weight, up_weight, down_weight, target_basis):
    token_count, feature_width = tokens.shape
    pick_count = expert_ids.shape[1]
    owner_count = lax.axis_size("expert")
    expert_count = owner_count // SLICES
    capacity = min(token_count, max(2, 5 * token_count * pick_count // (4 * expert_count)))
    rank_width = target_basis.shape[1]
    flat_ids = expert_ids.reshape(-1)
    onehot = (flat_ids[:, None] == jnp.arange(expert_count, dtype=jnp.int32)[None, :]).astype(
        jnp.int32
    )
    before = jnp.cumsum(onehot, axis=0) - onehot
    slot_rank = jnp.sum(before * onehot, axis=1)
    slot_index = flat_ids * capacity + slot_rank
    row_token = jnp.arange(token_count * pick_count, dtype=jnp.int32) // pick_count
    slot_table = (
        jnp.full((expert_count * capacity,), token_count, jnp.int32).at[slot_index].set(row_token)
    )
    padded = jnp.concatenate([tokens, jnp.zeros((1, feature_width), tokens.dtype)], axis=0)
    per_expert_rows = padded[slot_table].reshape(expert_count, 1, capacity, feature_width)
    outgoing = jnp.broadcast_to(per_expert_rows, (expert_count, SLICES, capacity, feature_width))
    outgoing = outgoing.reshape(owner_count, capacity, feature_width)
    full_basis = lax.all_gather(target_basis, "expert", axis=0, tiled=True)
    expert_part = run_expert(
        lax.all_to_all(outgoing, "expert", split_axis=0, concat_axis=0, tiled=True),
        gate_weight,
        up_weight,
        down_weight,
    )
    result = jnp.einsum("skd,dr->skr", expert_part, full_basis, preferred_element_type=jnp.float32)
    returned = lax.all_to_all(result, "expert", split_axis=0, concat_axis=0, tiled=True)
    summed = jnp.sum(returned.reshape(expert_count, SLICES, capacity, rank_width), axis=1)
    projected = summed.reshape(expert_count * capacity, rank_width)[slot_index]
    codes_float = gate_codes.astype(jnp.float32)
    weights = 2.5 * codes_float / jnp.sum(codes_float, axis=1, keepdims=True)
    projected = projected.reshape(token_count, pick_count, rank_width)
    return jnp.sum(weights[:, :, None] * projected, axis=1).astype(jnp.bfloat16)


def solution(mesh):
    in_specs = (
        P(("group", "expert"), None),
        P(("group", "expert"), None),
        P(("group", "expert"), None),
        P("expert", None, None),
        P("expert", None, None),
        P("expert", None, None),
        P("expert", None),
    )
    out_specs = P(("group", "expert"), None)
    return jax.shard_map(shards, mesh=mesh, in_specs=in_specs, out_specs=out_specs, check_vma=False)
```

profile of v0, /device:TPU:0, one launch (start us, length us, event | category | flops | bytes accessed | tf_op | source)
XLA Modules:
  0.0 122.3 jit_solution(8186890199680378276)
XLA Ops:
  6.5 0.7 all-gather.2.cloned.1.call-update
  7.3 0.8 copy.25
  8.1 0.7 broadcast_multiply_fusion
  8.8 0.1 copy.24
  8.9 0.1 mul.37
  9.0 0.2 reduce_window_sum.11
  9.2 0.8 concatenate.3
  10.1 0.6 scatter_custom_fusion
  10.7 0.6 gather_fusion
  11.4 1.2 broadcast_in_dim.8
  12.5 7.4 %all-to-all-start = ((bf16[16,4,7168]{2,1,0:T(4,128)(2,1)}), bf16[16,4,7168]{2,1,0:T(4,128)(2,1)S(1)}, u32[]{:S(2)}, u32[]{:S(2)}) async-start(bf16[16,4,7168]{2,1,0:T(4,128)(2,1)} %bitcast.2), calls=%async_computation | async-start | bytes 1835008 | tf_op jit(solution)/shard_map/all_to_all | solution.py:45
  19.9 35.3 %all-to-all-done = bf16[16,4,7168]{2,1,0:T(4,128)(2,1)S(1)} async-done(((bf16[16,4,7168]{2,1,0:T(4,128)(2,1)}), bf16[16,4,7168]{2,1,0:T(4,128)(2,1)S(1)}, u32[]{:S(2)}, u32[]{:S(2)}) %all-to-all-start) | async-done | bytes 917536 | tf_op jit(solution)/shard_map/all_to_all | solution.py:45
  55.2 0.2 reshape.53
  55.4 2.8 %fusion.5 = f32[64,256]{1,0:T(8,128)S(1)} fusion(bf16[64,7168]{1,0:T(8,128)(2,1)S(1)} %reshape.53, bf16[1,7168,256]{2,1,0:T(8,128)(2,1)} %param.10), kind=kOutput, calls=%fused_computation.9 | convolution fusion | flops 234881024 | bytes 4653056 | tf_op jit(solution)/shard_map/dot_general | solution.py:12
  58.2 5.6 %convolution_convert_fusion = bf16[64,7168]{1,0:T(8,128)(2,1)S(1)} fusion(bf16[1,256,7168]{2,1,0:T(8,128)(2,1)} %param.12, bf16[64,7168]{1,0:T(8,128)(2,1)S(1)} %reshape.53, bf16[1,7168,256]{2,1,0:T(8,128)(2,1)} %param.11, f32[64,256]{1,0:T(8,128)S(1)} %fusion.5), kind=kOutput, calls=%fused_computation.3 | convolution fusion | flops 470319104 | bytes 9240576 | tf_op jit(solution)/shard_map/dot_general | solution.py:15
  63.8 0.3 reshape.54
  64.2 33.6 %all-gather.2.cloned.1.call-done = bf16[7168,512]{1,0:T(8,128)(2,1)} async-done(((bf16[448,512]{1,0:T(8,128)(2,1)}), bf16[7168,512]{1,0:T(8,128)(2,1)}) %all-gather.2.cloned.1.call-update) | async-done | bytes 7340048 | tf_op jit(solution)/shard_map/all_gather | solution.py:43
  97.8 4.2 %fusion = f32[16,4,512]{2,0,1:T(8,128)S(1)} fusion(bf16[7168,512]{1,0:T(8,128)(2,1)} %all-gather.2.cloned.1.call-done, bf16[16,4,7168]{2,1,0:T(4,128)(2,1)S(1)} %reshape.54), kind=kOutput, calls=%fused_computation.4 | convolution fusion | flops 469762048 | bytes 8388608 | tf_op jit(solution)/shard_map/skd,dr->skr/dot_general | solution.py:50
  102.0 0.7 copy.27
  102.7 3.5 %all-to-all-start.1 = ((f32[16,4,512]{2,1,0:T(4,128)}), f32[16,4,512]{2,1,0:T(4,128)S(1)}, u32[]{:S(2)}, u32[]{:S(2)}) async-start(f32[16,4,512]{2,1,0:T(4,128)} %copy.27), calls=%async_computation.1 | async-start | bytes 262144 | tf_op jit(solution)/shard_map/all_to_all | solution.py:51
  106.3 0.1 copy.23
  106.4 7.8 %all-to-all-done.1 = f32[16,4,512]{2,1,0:T(4,128)S(1)} async-done(((f32[16,4,512]{2,1,0:T(4,128)}), f32[16,4,512]{2,1,0:T(4,128)S(1)}, u32[]{:S(2)}, u32[]{:S(2)}) %all-to-all-start.1) | async-done | bytes 131104 | tf_op jit(solution)/shard_map/all_to_all | solution.py:51
  114.2 0.6 gather_fusion.1
  114.8 0.7 multiply_reduce_fusion
  (17 shorter events, 0.3 us)
Async XLA Ops:
  6.5 13.4 %copy-start = (s32[4,2]{0,1:T(2,128)S(1)}, s32[4,2]{0,1:T(2,128)}, u32[]{:S(2)}) copy-start(s32[4,2]{0,1:T(2,128)} %param.9) | copy-start | bytes 100
  6.5 91.2 %all-gather.2.cloned.1.call-start = ((), (), s32[]{:S(2)}) async-start(), calls=%async_computation.2 | async-start | bytes 7798784 | tf_op jit(solution)/shard_map/all_gather | solution.py:43
  12.5 42.7 %all-to-all-start = ((bf16[16,4,7168]{2,1,0:T(4,128)(2,1)}), bf16[16,4,7168]{2,1,0:T(4,128)(2,1)S(1)}, u32[]{:S(2)}, u32[]{:S(2)}) async-start(bf16[16,4,7168]{2,1,0:T(4,128)(2,1)} %bitcast.2), calls=%async_computation | async-start | bytes 1835008 | tf_op jit(solution)/shard_map/all_to_all | solution.py:45
  102.7 11.4 %all-to-all-start.1 = ((f32[16,4,512]{2,1,0:T(4,128)}), f32[16,4,512]{2,1,0:T(4,128)S(1)}, u32[]{:S(2)}, u32[]{:S(2)}) async-start(f32[16,4,512]{2,1,0:T(4,128)} %copy.27), calls=%async_computation.1 | async-start | bytes 262144 | tf_op jit(solution)/shard_map/all_to_all | solution.py:51
Sparse Core Ops, SparseCore 0:
  9.6 88.0 all-gather.1
where the time goes:
time: 123 us; the launch traced here: 122 us
  waiting for transfers between devices  77.4 us (63%)
  between operations  13.5 us (11%)
  matrix products  12.6 us (10%)
  starting transfers between devices  10.9 us (9%)
  local copies, waits for them, and re-layouts  6.26 us (5%)
  other arithmetic  1.66 us (1%)
    all_to_all x1, waiting for transfers between devices, shards(): lax.all_to_all(outgoing, 'expert', split_axis=0, concat_axis=0, tiled=True)  35.3 us
    all_gather x1, waiting for transfers between devices, shards(): full_basis = lax.all_gather(target_basis, 'expert', axis=0, tiled=True)  33.6 us
    all_to_all x1, waiting for transfers between devices, shards(): lax.all_to_all(result, 'expert', split_axis=0, concat_axis=0, tiled=True)  7.78 us
    all_to_all x1, starting transfers between devices, shards(): lax.all_to_all(outgoing, 'expert', split_axis=0, concat_axis=0, tiled=True)  7.39 us
    dot_general x1, matrix products, run_expert(): jnp.dot(hidden, down_weight[0], preferred_element_type=jnp.float32)  5.61 us
    dot_general x1, matrix products, shards(): jnp.einsum('skd,dr->skr', expert_part, full_basis, preferred_element_type...  4.22 us
    all_to_all x1, starting transfers between devices, shards(): lax.all_to_all(result, 'expert', split_axis=0, concat_axis=0, tiled=True)  3.51 us
    dot_general x1, matrix products, run_expert(): jnp.dot(row_block, gate_weight[0], preferred_element_type=jnp.float32)  2.75 us
  transfers between devices with their start and end apart: 3, of which 3 were waited for; matrix products, arithmetic and copies ran while one was open for 12% of the time, Pallas kernels for 0%

commit v1 on v0

--- a/solution.py
+++ b/solution.py
@@ -1,9 +1,16 @@
+import functools
+
 import jax
 import jax.numpy as jnp
 from jax import lax
+from jax.experimental import pallas as pl
+from jax.experimental.pallas import tpu as pltpu
 from jax.sharding import PartitionSpec as P
 
 SLICES = 8
+LANES = 128
+ROWS = 16
+MESH = pl.DeviceIdType.MESH
 
 
 def run_expert(received, gate_weight, up_weight, down_weight):
@@ -18,7 +25,7 @@
     return expert_part.reshape(sources, slots, feature_width)
 
 
-def shards(tokens, expert_ids, gate_codes, gate_weight, up_weight, down_weight, target_basis):
+def gathered(tokens, expert_ids, gate_codes, gate_weight, up_weight, down_weight, target_basis):
     token_count, feature_width = tokens.shape
     pick_count = expert_ids.shape[1]
     owner_count = lax.axis_size("expert")
@@ -26,13 +33,11 @@
     capacity = min(token_count, max(2, 5 * token_count * pick_count // (4 * expert_count)))
     rank_width = target_basis.shape[1]
     flat_ids = expert_ids.reshape(-1)
-    onehot = (flat_ids[:, None] == jnp.arange(expert_count, dtype=jnp.int32)[None, :]).astype(
-        jnp.int32
-    )
-    before = jnp.cumsum(onehot, axis=0) - onehot
-    slot_rank = jnp.sum(before * onehot, axis=1)
+    order = jnp.arange(token_count * pick_count, dtype=jnp.int32)
+    same = (flat_ids[:, None] == flat_ids[None, :]) & (order[None, :] < order[:, None])
+    slot_rank = jnp.sum(same.astype(jnp.int32), axis=1)
     slot_index = flat_ids * capacity + slot_rank
-    row_token = jnp.arange(token_count * pick_count, dtype=jnp.int32) // pick_count
+    row_token = order // pick_count
     slot_table = (
         jnp.full((expert_count * capacity,), token_count, jnp.int32).at[slot_index].set(row_token)
     )
@@ -57,6 +62,247 @@
     return jnp.sum(weights[:, :, None] * projected, axis=1).astype(jnp.bfloat16)
 
 
+def kernel(
+    n, tok, ids, codes, gw, uw, dw, basis, out,
+    wg, wu, wd, bs, x, accg, accu, ypart, yexch, yout, yrecv, zsend, zrecv,
+    w_sem, b_sem, own_send, fwd_send, x_recv, e_send, e_recv, y_send, y_recv, z_send, z_recv,
+):
+    f32, bf16 = jnp.float32, jnp.bfloat16
+    count, width = tok.shape
+    parts = ROWS // count
+    piece = width // parts
+    chips = n // 2
+    half = n * count // 2
+    block = width // chips
+    experts = n // SLICES
+    me = lax.axis_index("expert")
+    chip, core = me // 2, me % 2
+    sib = chip * 2 + 1 - core
+    my_half = me // chips
+
+    def remote(src, dst, ssem, rsem, dev):
+        return pltpu.make_async_remote_copy(
+            src_ref=src, dst_ref=dst, send_sem=ssem, recv_sem=rsem,
+            device_id={"expert": dev}, device_id_type=MESH,
+        )
+
+    loads = [
+        pltpu.make_async_copy(src.at[0], dst, w_sem.at[i])
+        for i, (src, dst) in enumerate(((gw, wg), (uw, wu), (dw, wd)))
+    ]
+    for load in loads:
+        load.start()
+    barrier = pltpu.get_barrier_semaphore()
+    for k in range(1, n):
+        pl.semaphore_signal(barrier, inc=1, device_id={"expert": (me + k) % n}, device_id_type=MESH)
+
+    lane = lax.broadcasted_iota(jnp.int32, (count, LANES), 1)
+    picked = codes[...].astype(f32)
+    weights = 2.5 * picked / jnp.sum(picked, axis=1, keepdims=True)
+    named = ids[...]
+    both = jnp.zeros((count, LANES), f32)
+    for k in range(named.shape[1]):
+        e = named[:, k : k + 1]
+        both += jnp.where((lane == e) | (lane == e + experts), weights[:, k : k + 1], 0.0)
+    high = both.astype(bf16).astype(f32)
+    extra = jnp.where(lane < experts, high, both - high)
+    rows = tok[...].astype(f32)
+    own = jnp.concatenate(
+        [
+            jnp.concatenate([rows[:, q * piece : (q + 1) * piece], extra], axis=1)
+            for q in range(parts)
+        ],
+        axis=0,
+    )
+    x[me] = own.astype(bf16)
+    pl.semaphore_wait(barrier, n - 1)
+
+    sends = []
+    for k in range(1, chips):
+        c = remote(x.at[me], x.at[me], own_send.at[k], x_recv.at[me], ((chip + k) % chips) * 2 + core)
+        c.start()
+        sends.append(c)
+    c = remote(x.at[me], x.at[me], fwd_send.at[0], x_recv.at[me], sib)
+    c.start()
+    sends.append(c)
+    cb = remote(basis, bs.at[core], b_sem.at[0], b_sem.at[1], sib)
+    cb.start()
+    bs[core] = basis[...]
+    for k in range(1, chips):
+        src = ((chip + k) % chips) * 2 + core
+        remote(x.at[src], x.at[src], own_send.at[0], x_recv.at[src], sib).wait_recv()
+        c = remote(x.at[src], x.at[src], fwd_send.at[k], x_recv.at[src], sib)
+        c.start()
+        sends.append(c)
+    for k in range(chips):
+        src = ((chip + k) % chips) * 2 + 1 - core
+        remote(x.at[src], x.at[src], own_send.at[0], x_recv.at[src], sib).wait_recv()
+    loads[0].wait()
+    loads[1].wait()
+
+    total = n * ROWS
+    place = lax.broadcasted_iota(jnp.int32, (total, 1), 0) % ROWS // count
+    left = x[:, :, 0:piece].reshape(total, piece)
+
+    def part(q, carry):
+        at = pl.ds(pl.multiple_of(q * piece, LANES), piece)
+        g = jnp.dot(left, wg[at, :], preferred_element_type=f32)
+        accg[...] = jnp.where(place == q, g, accg[...])
+        u = jnp.dot(left, wu[at, :], preferred_element_type=f32)
+        accu[...] = jnp.where(place == q, u, accu[...])
+        return carry
+
+    accg[...] = jnp.zeros_like(accg)
+    accu[...] = jnp.zeros_like(accu)
+    lax.fori_loop(0, parts, part, 0)
+
+    def fold(v):
+        step = count
+        while step < ROWS:
+            v = v + pltpu.roll(v, total - step, 0)
+            step *= 2
+        return v
+
+    g, u = fold(accg[...]), fold(accu[...])
+    tail = x[:, :, piece:].reshape(total, LANES).astype(f32)
+    lane = lax.broadcasted_iota(jnp.int32, (total, LANES), 1)
+    mine = me // SLICES
+    weight = jnp.sum(
+        jnp.where((lane == mine) | (lane == mine + experts), tail, 0.0), axis=1, keepdims=True
+    )
+    hidden = (g / (1.0 + jnp.exp(-g)) * u * weight).astype(bf16)
+    i = lax.broadcasted_iota(jnp.int32, (n * count, total), 0)
+    j = lax.broadcasted_iota(jnp.int32, (n * count, total), 1)
+    pick = jnp.where(j == i // count * ROWS + i % count, 1.0, 0.0).astype(bf16)
+    hidden = jnp.dot(pick, hidden, preferred_element_type=f32).astype(bf16)
+
+    loads[2].wait()
+    for k in range(chips):
+        to = (chip + 1 + k) % chips
+        y = jnp.dot(
+            hidden,
+            wd[:, pl.ds(pl.multiple_of(to * block, LANES), block)],
+            preferred_element_type=f32,
+        ).astype(bf16)
+        ypart[to] = y.reshape(2, half, block)
+        c = remote(ypart.at[to, 1 - core], yexch.at[to], e_send.at[to], e_recv.at[to], sib)
+        c.start()
+        sends.append(c)
+    for k in range(chips):
+        to = (chip + 1 + k) % chips
+        remote(yexch.at[to], yexch.at[to], e_send.at[to], e_recv.at[to], sib).wait_recv()
+        summed = ypart[to, core].astype(f32) + yexch[to].astype(f32)
+        if k == chips - 1:
+            z = summed
+        else:
+            yout[to] = summed.astype(bf16)
+            c = remote(yout.at[to], yrecv.at[chip], y_send.at[to], y_recv.at[chip], to * 2 + core)
+            c.start()
+            sends.append(c)
+    for k in range(1, chips):
+        src = (chip + chips - k) % chips
+        remote(yrecv.at[src], yrecv.at[src], y_send.at[src], y_recv.at[src], sib).wait_recv()
+        z = z + yrecv[src].astype(f32)
+
+    cb.wait()
+    full = bs[...].reshape(block, basis.shape[1])
+    p = jnp.dot(z.astype(bf16), full, preferred_element_type=f32)
+    for d in range(chips):
+        zsend[d] = p[d * count : (d + 1) * count]
+    for k in range(chips):
+        d = (me + k) % chips
+        c = remote(zsend.at[d], zrecv.at[chip], z_send.at[k], z_recv.at[chip], core * chips + d)
+        if k == 0:
+
+            @pl.when(my_half == core)
+            def _():
+                zrecv[chip] = zsend[d]
+
+            @pl.when(my_half != core)
+            def _():
+                c.start()
+                c.wait_send()
+        else:
+            c.start()
+            sends.append(c)
+    for src in range(chips):
+
+        @pl.when(src * 2 + my_half != me)
+        def _():
+            remote(zrecv.at[src], zrecv.at[src], z_send.at[0], z_recv.at[src], sib).wait_recv()
+
+    out[...] = jnp.sum(zrecv[...], axis=0).astype(bf16)
+    for c in sends:
+        c.wait_send()
+
+
+def fused(tokens, expert_ids, gate_codes, gate_weight, up_weight, down_weight, target_basis):
+    n = lax.axis_size("expert")
+    count, width = tokens.shape
+    unit = gate_weight.shape[2]
+    rank = target_basis.shape[1]
+    chips, half = n // 2, n * count // 2
+    block = width // chips
+    piece = width * count // ROWS
+    bf16, f32 = jnp.bfloat16, jnp.float32
+    dma = pltpu.SemaphoreType.DMA
+    vmem = pl.BlockSpec(memory_space=pltpu.VMEM)
+    hbm = pl.BlockSpec(memory_space=pl.ANY)
+    return pl.pallas_call(
+        functools.partial(kernel, n),
+        out_shape=jax.ShapeDtypeStruct((count, rank), bf16),
+        in_specs=[vmem, vmem, vmem, hbm, hbm, hbm, vmem],
+        out_specs=vmem,
+        scratch_shapes=[
+            pltpu.VMEM((width, unit), bf16),
+            pltpu.VMEM((width, unit), bf16),
+            pltpu.VMEM((unit, width), bf16),
+            pltpu.VMEM((2, width // n, rank), bf16),
+            pltpu.VMEM((n, ROWS, piece + LANES), bf16),
+            pltpu.VMEM((n * ROWS, unit), f32),
+            pltpu.VMEM((n * ROWS, unit), f32),
+            pltpu.VMEM((chips, 2, half, block), bf16),
+            pltpu.VMEM((chips, half, block), bf16),
+            pltpu.VMEM((chips, half, block), bf16),
+            pltpu.VMEM((chips, half, block), bf16),
+            pltpu.VMEM((chips, count, rank), f32),
+            pltpu.VMEM((chips, count, rank), f32),
+            dma((3,)),
+            dma((2,)),
+            dma((chips,)),
+            dma((chips,)),
+            dma((n,)),
+            dma((chips,)),
+            dma((chips,)),
+            dma((chips,)),
+            dma((chips,)),
+            dma((chips,)),
+            dma((chips,)),
+        ],
+        compiler_params=pltpu.CompilerParams(
+            collective_id=0, has_side_effects=True, vmem_limit_bytes=40 * 2**20
+        ),
+    )(tokens, expert_ids, gate_codes, gate_weight, up_weight, down_weight, target_basis)
+
+
+def shards(tokens, expert_ids, gate_codes, gate_weight, up_weight, down_weight, target_basis):
+    n = lax.axis_size("expert")
+    count, width = tokens.shape
+    fits = (
+        n % 2 == 0
+        and ROWS % count == 0
+        and width * count % (ROWS * LANES) == 0
+        and (n * count) % (2 * ROWS) == 0
+        and width % (n // 2 * LANES) == 0
+        and width // n % ROWS == 0
+        and 2 * (n // SLICES) <= LANES
+    )
+    run = fused if fits else gathered
+    return run(
+        tokens, expert_ids, gate_codes, gate_weight, up_weight, down_weight, target_basis
+    )
+
+
 def solution(mesh):
     in_specs = (
         P(("group", "expert"), None),

time: 123 us -> 55.4 us (0.45)
  waiting for transfers between devices: 77.4 us -> 0 us
  Pallas kernels: 0 us -> 45 us
  between operations: 13.5 us -> 0.02 us
  matrix products: 12.6 us -> 0 us
  starting transfers between devices: 10.9 us -> 0 us
  local copies, waits for them, and re-layouts: 6.26 us -> 10.1 us
  other arithmetic: 1.66 us -> 0 us
    pallas_call x0 -> x1, Pallas kernels: none -> 45 us  [fused(): pl.pallas_call(functools.partial(kernel, n), out_shape=jax.ShapeDtypeStru...]
    all_to_all x2 -> x0, waiting for transfers between devices: 43.1 us -> none  [the longest x1 35.3 us: shards(): lax.all_to_all(outgoing, 'expert', split_axis=0, concat_axis=0, tiled=True)]
    all_gather x1 -> x0, waiting for transfers between devices: 33.6 us -> none  [shards(): full_basis = lax.all_gather(target_basis, 'expert', axis=0, tiled=True)]
    dot_general x3 -> x0, matrix products: 12.6 us -> none  [the longest x1 5.61 us: run_expert(): jnp.dot(hidden, down_weight[0], preferred_element_type=jnp.float32)]
    all_to_all x2 -> x0, starting transfers between devices: 10.9 us -> none  [the longest x1 7.39 us: shards(): lax.all_to_all(outgoing, 'expert', split_axis=0, concat_axis=0, tiled=True)]
    unnamed x3 -> x13, local copies, waits for them, and re-layouts: 0.77 us -> 10.1 us
  transfers between devices with their start and end apart: 3 -> 0, of which waited for: 3 -> 0; matrix products, arithmetic and copies ran while one was open for 12% -> 0% of each run, Pallas kernels for 0% -> 0%
where the time goes in v1:
time: 55.4 us; the launch traced here: 55.1 us
  Pallas kernels  45 us (81%)
  local copies, waits for them, and re-layouts  10.1 us (18%)
    pallas_call x1, Pallas kernels, fused(): pl.pallas_call(functools.partial(kernel, n), out_shape=jax.ShapeDtypeStru...  45 us
    unnamed x13, local copies, waits for them, and re-layouts  10.1 us

profile of v1, /device:TPU:0, one launch (start us, length us, event | category | flops | bytes accessed | tf_op | source)
XLA Modules:
  0.0 55.1 jit_solution(16205857119154136475)
XLA Ops:
  0.0 0.8 %copy.8.ids = s32[4,2]{1,0:T(4,128)S(1)} copy(s32[4,2]{0,1:T(2,128)} %param.8) | data formatting | bytes 64 | tf_op args[1]
  0.8 0.8 %copy.9.codes = s32[4,2]{1,0:T(4,128)S(1)} copy(s32[4,2]{0,1:T(2,128)} %param.9) | data formatting | bytes 64 | tf_op args[2]
  1.5 0.0 copy-start
  1.5 2.0 %copy-done = bf16[1,7168,256]{2,1,0:T(8,128)(2,1)S(1)} copy-done((bf16[1,7168,256]{2,1,0:T(8,128)(2,1)S(1)}, bf16[1,7168,256]{2,1,0:T(8,128)(2,1)}, u32[]{:S(2)}) %copy-start) | copy-done | bytes 3670040
  3.6 0.0 copy-start.1
  3.6 2.0 %copy-done.1 = bf16[1,7168,256]{2,1,0:T(8,128)(2,1)S(1)} copy-done((bf16[1,7168,256]{2,1,0:T(8,128)(2,1)S(1)}, bf16[1,7168,256]{2,1,0:T(8,128)(2,1)}, u32[]{:S(2)}) %copy-start.1) | copy-done | bytes 3670040
  5.6 0.0 copy-start.2
  5.6 2.0 %copy-done.2 = bf16[1,256,7168]{2,1,0:T(8,128)(2,1)S(1)} copy-done((bf16[1,256,7168]{2,1,0:T(8,128)(2,1)S(1)}, bf16[1,256,7168]{2,1,0:T(8,128)(2,1)}, u32[]{:S(2)}) %copy-start.2) | copy-done | bytes 3670040
  7.6 0.0 copy-start.3
  7.6 1.0 %copy-done.3 = bf16[448,512]{1,0:T(8,128)(2,1)S(1)} copy-done((bf16[448,512]{1,0:T(8,128)(2,1)S(1)}, bf16[448,512]{1,0:T(8,128)(2,1)}, u32[]{:S(2)}) %copy-start.3) | copy-done | bytes 458776
  8.7 0.0 copy-start.4
  8.7 0.8 %copy-done.4 = bf16[4,7168]{1,0:T(4,128)(2,1)S(1)} copy-done((bf16[4,7168]{1,0:T(4,128)(2,1)S(1)}, bf16[4,7168]{1,0:T(4,128)(2,1)}, u32[]{:S(2)}) %copy-start.4) | copy-done | bytes 57368
  9.5 45.0 %shard_map.73 = bf16[4,512]{1,0:T(4,128)(2,1)S(1)} custom-call(bf16[4,7168]{1,0:T(4,128)(2,1)S(1)} %copy-done.4, s32[4,2]{1,0:T(4,128)S(1)} %copy.8.ids, s32[4,2]{1,0:T(4,128)S(1)} %copy.9.codes, bf16[1,7168,256]{2,1,0:T(8,128)(2,1)S(1)} %copy-done, bf16[1,7168,256]{2,1,0:T(8,128)(2,1)S(1)} %copy-done.1, bf16[1,256,7168]{2,1,0:T(8,128)(2,1)S(1)} %copy-done.2, ...), custom_call_target="tpu_custom_call" | custom-call | tf_op jit(solution)/shard_map/pallas_call | solution.py:251
  54.5 0.6 %copy.11 = bf16[4,512]{1,0:T(4,128)(2,1)} copy(bf16[4,512]{1,0:T(4,128)(2,1)S(1)} %shard_map.73) | data formatting | bytes 8192
Async XLA Ops:
  1.5 2.0 %copy-start = (bf16[1,7168,256]{2,1,0:T(8,128)(2,1)S(1)}, bf16[1,7168,256]{2,1,0:T(8,128)(2,1)}, u32[]{:S(2)}) copy-start(bf16[1,7168,256]{2,1,0:T(8,128)(2,1)} %gw.1) | copy-start | bytes 11010052
  3.6 2.0 %copy-start.1 = (bf16[1,7168,256]{2,1,0:T(8,128)(2,1)S(1)}, bf16[1,7168,256]{2,1,0:T(8,128)(2,1)}, u32[]{:S(2)}) copy-start(bf16[1,7168,256]{2,1,0:T(8,128)(2,1)} %uw.1) | copy-start | bytes 11010052
  5.6 2.0 %copy-start.2 = (bf16[1,256,7168]{2,1,0:T(8,128)(2,1)S(1)}, bf16[1,256,7168]{2,1,0:T(8,128)(2,1)}, u32[]{:S(2)}) copy-start(bf16[1,256,7168]{2,1,0:T(8,128)(2,1)} %dw.1) | copy-start | bytes 11010052
  7.6 1.0 %copy-start.3 = (bf16[448,512]{1,0:T(8,128)(2,1)S(1)}, bf16[448,512]{1,0:T(8,128)(2,1)}, u32[]{:S(2)}) copy-start(bf16[448,512]{1,0:T(8,128)(2,1)} %basis.1) | copy-start | bytes 1376260
  8.7 0.8 %copy-start.4 = (bf16[4,7168]{1,0:T(4,128)(2,1)S(1)}, bf16[4,7168]{1,0:T(4,128)(2,1)}, u32[]{:S(2)}) copy-start(bf16[4,7168]{1,0:T(4,128)(2,1)} %tok.1) | copy-start | bytes 172036

commit v2 on v1

--- a/solution.py
+++ b/solution.py
@@ -63,9 +63,9 @@
 
 
 def kernel(
-    n, tok, ids, codes, gw, uw, dw, basis, out,
-    wg, wu, wd, bs, x, accg, accu, ypart, yexch, yout, yrecv, zsend, zrecv,
-    w_sem, b_sem, own_send, fwd_send, x_recv, e_send, e_recv, y_send, y_recv, z_send, z_recv,
+    n, tok_in, ids, codes, gw, uw, dw, basis, out,
+    tok, wg, wu, wd, bs, x, accg, accu, yown, ypart, yexch, yout, yrecv, zsend, zrecv,
+    w_sem, b_sem, own_send, side_send, fwd_send, x_recv, e_send, e_recv, y_send, y_recv, z_send, z_recv,
 ):
     f32, bf16 = jnp.float32, jnp.bfloat16
     count, width = tok.shape
@@ -78,7 +78,13 @@
     me = lax.axis_index("expert")
     chip, core = me // 2, me % 2
     sib = chip * 2 + 1 - core
-    my_half = me // chips
+    across = 2 - chips % 2
+    along = chips // across
+    a, b = chip // across, chip % across
+
+    def at(a, b, c):
+        return (a % along * across + b % across) * 2 + c
+
 
     def remote(src, dst, ssem, rsem, dev):
         return pltpu.make_async_remote_copy(
@@ -86,26 +92,42 @@
             device_id={"expert": dev}, device_id_type=MESH,
         )
 
+    first = pltpu.make_async_copy(tok_in, tok, w_sem.at[3])
+    first.start()
     loads = [
         pltpu.make_async_copy(src.at[0], dst, w_sem.at[i])
         for i, (src, dst) in enumerate(((gw, wg), (uw, wu), (dw, wd)))
     ]
+    barrier = pltpu.get_barrier_semaphore()
+    for peer in [sib] + [((chip + k) % chips) * 2 + core for k in range(1, chips)]:
+        pl.semaphore_signal(barrier, inc=1, device_id={"expert": peer}, device_id_type=MESH)
+
     for load in loads:
         load.start()
-    barrier = pltpu.get_barrier_semaphore()
-    for k in range(1, n):
-        pl.semaphore_signal(barrier, inc=1, device_id={"expert": (me + k) % n}, device_id_type=MESH)
-
+    mb = pltpu.make_async_copy(basis, bs.at[core], b_sem.at[2])
+    mb.start()
     lane = lax.broadcasted_iota(jnp.int32, (count, LANES), 1)
     picked = codes[...].astype(f32)
-    weights = 2.5 * picked / jnp.sum(picked, axis=1, keepdims=True)
-    named = ids[...]
+    weights = 2.5 * picked / jnp.sum(picked, axis=0, keepdims=True)
+    named = ids[...].astype(f32)
+    square = (count, count)
+    diagonal = lax.broadcasted_iota(jnp.int32, square, 0) == lax.broadcasted_iota(
+        jnp.int32, square, 1
+    )
+
+    def column(row):
+        return jnp.sum(
+            jnp.where(diagonal, jnp.broadcast_to(row, square), 0.0), axis=1, keepdims=True
+        )
+
     both = jnp.zeros((count, LANES), f32)
-    for k in range(named.shape[1]):
-        e = named[:, k : k + 1]
-        both += jnp.where((lane == e) | (lane == e + experts), weights[:, k : k + 1], 0.0)
+    for k in range(named.shape[0]):
+        e = column(named[k : k + 1])
+        spot = lane.astype(f32)
+        both += jnp.where((spot == e) | (spot == e + experts), column(weights[k : k + 1]), 0.0)
     high = both.astype(bf16).astype(f32)
     extra = jnp.where(lane < experts, high, both - high)
+    first.wait()
     rows = tok[...].astype(f32)
     own = jnp.concatenate(
         [
@@ -115,28 +137,40 @@
         axis=0,
     )
     x[me] = own.astype(bf16)
-    pl.semaphore_wait(barrier, n - 1)
+    pl.semaphore_wait(barrier, chips)
 
     sends = []
-    for k in range(1, chips):
-        c = remote(x.at[me], x.at[me], own_send.at[k], x_recv.at[me], ((chip + k) % chips) * 2 + core)
+
+    def pass_on(src, sem, dev):
+        c = remote(x.at[src], x.at[src], sem, x_recv.at[src], dev)
         c.start()
         sends.append(c)
-    c = remote(x.at[me], x.at[me], fwd_send.at[0], x_recv.at[me], sib)
-    c.start()
-    sends.append(c)
+
+    def arrived(src):
+        remote(x.at[src], x.at[src], own_send.at[0], x_recv.at[src], sib).wait_recv()
+
+    steps = [k for k in (1, along - 1) if 0 < k < along]
+    steps = list(dict.fromkeys(steps + list(range(1, along))))
+    for k in steps:
+        pass_on(me, own_send.at[k], at(a + k, b, core))
+    if across == 2:
+        pass_on(me, side_send.at[0], at(a, b + 1, core))
+    pass_on(me, fwd_send.at[0], sib)
+    for k in steps:
+        src = at(a + along - k, b, core)
+        arrived(src)
+        if across == 2:
+            pass_on(src, side_send.at[k], at(a, b + 1, core))
+        pass_on(src, fwd_send.at[k], sib)
+    if across == 2:
+        for k in [0] + steps:
+            src = at(a + along - k, b + 1, core)
+            arrived(src)
+            pass_on(src, fwd_send.at[along + k], sib)
     cb = remote(basis, bs.at[core], b_sem.at[0], b_sem.at[1], sib)
     cb.start()
-    bs[core] = basis[...]
-    for k in range(1, chips):
-        src = ((chip + k) % chips) * 2 + core
-        remote(x.at[src], x.at[src], own_send.at[0], x_recv.at[src], sib).wait_recv()
-        c = remote(x.at[src], x.at[src], fwd_send.at[k], x_recv.at[src], sib)
-        c.start()
-        sends.append(c)
     for k in range(chips):
-        src = ((chip + k) % chips) * 2 + 1 - core
-        remote(x.at[src], x.at[src], own_send.at[0], x_recv.at[src], sib).wait_recv()
+        arrived(((chip + k) % chips) * 2 + 1 - core)
     loads[0].wait()
     loads[1].wait()
 
@@ -145,10 +179,10 @@
     left = x[:, :, 0:piece].reshape(total, piece)
 
     def part(q, carry):
-        at = pl.ds(pl.multiple_of(q * piece, LANES), piece)
-        g = jnp.dot(left, wg[at, :], preferred_element_type=f32)
+        span = pl.ds(pl.multiple_of(q * piece, LANES), piece)
+        g = jnp.dot(left, wg[span, :], preferred_element_type=f32)
         accg[...] = jnp.where(place == q, g, accg[...])
-        u = jnp.dot(left, wu[at, :], preferred_element_type=f32)
+        u = jnp.dot(left, wu[span, :], preferred_element_type=f32)
         accu[...] = jnp.where(place == q, u, accu[...])
         return carry
 
@@ -164,72 +198,73 @@
         return v
 
     g, u = fold(accg[...]), fold(accu[...])
-    tail = x[:, :, piece:].reshape(total, LANES).astype(f32)
-    lane = lax.broadcasted_iota(jnp.int32, (total, LANES), 1)
+    hidden = (g / (1.0 + jnp.exp(-g)) * u).astype(bf16)
+    i = lax.broadcasted_iota(jnp.int32, (n * count, total), 0)
+    owner = i % half // count * 2 + (i // half + core) % 2
+    j = lax.broadcasted_iota(jnp.int32, (n * count, total), 1)
+    pick = jnp.where(j == owner * ROWS + i % count, 1.0, 0.0).astype(bf16)
+    hidden = jnp.dot(pick, hidden, preferred_element_type=f32).astype(bf16)
+    tail = x[:, :, piece:].reshape(total, LANES)
+    tail = jnp.dot(pick, tail, preferred_element_type=f32)
+    lane = lax.broadcasted_iota(jnp.int32, (n * count, LANES), 1)
     mine = me // SLICES
     weight = jnp.sum(
         jnp.where((lane == mine) | (lane == mine + experts), tail, 0.0), axis=1, keepdims=True
     )
-    hidden = (g / (1.0 + jnp.exp(-g)) * u * weight).astype(bf16)
-    i = lax.broadcasted_iota(jnp.int32, (n * count, total), 0)
-    j = lax.broadcasted_iota(jnp.int32, (n * count, total), 1)
-    pick = jnp.where(j == i // count * ROWS + i % count, 1.0, 0.0).astype(bf16)
-    hidden = jnp.dot(pick, hidden, preferred_element_type=f32).astype(bf16)
 
     loads[2].wait()
-    for k in range(chips):
-        to = (chip + 1 + k) % chips
-        y = jnp.dot(
-            hidden,
-            wd[:, pl.ds(pl.multiple_of(to * block, LANES), block)],
-            preferred_element_type=f32,
-        ).astype(bf16)
-        ypart[to] = y.reshape(2, half, block)
-        c = remote(ypart.at[to, 1 - core], yexch.at[to], e_send.at[to], e_recv.at[to], sib)
-        c.start()
-        sends.append(c)
-    for k in range(chips):
-        to = (chip + 1 + k) % chips
-        remote(yexch.at[to], yexch.at[to], e_send.at[to], e_recv.at[to], sib).wait_recv()
-        summed = ypart[to, core].astype(f32) + yexch[to].astype(f32)
-        if k == chips - 1:
-            z = summed
-        else:
-            yout[to] = summed.astype(bf16)
-            c = remote(yout.at[to], yrecv.at[chip], y_send.at[to], y_recv.at[chip], to * 2 + core)
+    z = None
+    lag = 2
+    for k in range(chips + lag):
+        if k < chips:
+            to = (chip + 1 + k) % chips
+            y = jnp.dot(
+                hidden,
+                wd[:, pl.ds(pl.multiple_of(to * block, LANES), block)],
+                preferred_element_type=f32,
+            )
+            y = y * weight
+            ypart[to] = y[half:].astype(bf16)
+            c = remote(ypart.at[to], yexch.at[to], e_send.at[to], e_recv.at[to], sib)
             c.start()
             sends.append(c)
+            yown[to] = y[:half]
+        if k >= lag:
+            to = (chip + 1 + k - lag) % chips
+            remote(yexch.at[to], yexch.at[to], e_send.at[to], e_recv.at[to], sib).wait_recv()
+            summed = yown[to] + yexch[to].astype(f32)
+            if k - lag == chips - 1:
+                z = summed
+            else:
+                yout[to] = summed.astype(bf16)
+                c = remote(
+                    yout.at[to], yrecv.at[chip], y_send.at[to], y_recv.at[chip], to * 2 + core
+                )
+                c.start()
+                sends.append(c)
     for k in range(1, chips):
         src = (chip + chips - k) % chips
         remote(yrecv.at[src], yrecv.at[src], y_send.at[src], y_recv.at[src], sib).wait_recv()
         z = z + yrecv[src].astype(f32)
 
     cb.wait()
+    mb.wait()
     full = bs[...].reshape(block, basis.shape[1])
-    p = jnp.dot(z.astype(bf16), full, preferred_element_type=f32)
+    coarse = z.astype(bf16)
+    fine = (z - coarse.astype(f32)).astype(bf16)
+    p = jnp.dot(jnp.concatenate([coarse, fine], axis=0), full, preferred_element_type=f32)
+    p = p[:half] + p[half:]
     for d in range(chips):
         zsend[d] = p[d * count : (d + 1) * count]
-    for k in range(chips):
-        d = (me + k) % chips
-        c = remote(zsend.at[d], zrecv.at[chip], z_send.at[k], z_recv.at[chip], core * chips + d)
-        if k == 0:
-
-            @pl.when(my_half == core)
-            def _():
-                zrecv[chip] = zsend[d]
-
-            @pl.when(my_half != core)
-            def _():
-                c.start()
-                c.wait_send()
-        else:
-            c.start()
-            sends.append(c)
-    for src in range(chips):
-
-        @pl.when(src * 2 + my_half != me)
-        def _():
-            remote(zrecv.at[src], zrecv.at[src], z_send.at[0], z_recv.at[src], sib).wait_recv()
+    for k in range(1, chips):
+        d = (chip + k) % chips
+        c = remote(zsend.at[d], zrecv.at[chip], z_send.at[k], z_recv.at[chip], d * 2 + core)
+        c.start()
+        sends.append(c)
+    zrecv[chip] = zsend[chip]
+    for k in range(1, chips):
+        src = (chip + chips - k) % chips
+        remote(zrecv.at[src], zrecv.at[src], z_send.at[0], z_recv.at[src], sib).wait_recv()
 
     out[...] = jnp.sum(zrecv[...], axis=0).astype(bf16)
     for c in sends:
@@ -247,13 +282,14 @@
     bf16, f32 = jnp.bfloat16, jnp.float32
     dma = pltpu.SemaphoreType.DMA
     vmem = pl.BlockSpec(memory_space=pltpu.VMEM)
-    hbm = pl.BlockSpec(memory_space=pl.ANY)
+    hbm = pl.BlockSpec(memory_space=pltpu.HBM)
     return pl.pallas_call(
         functools.partial(kernel, n),
         out_shape=jax.ShapeDtypeStruct((count, rank), bf16),
-        in_specs=[vmem, vmem, vmem, hbm, hbm, hbm, vmem],
+        in_specs=[hbm, vmem, vmem, hbm, hbm, hbm, hbm],
         out_specs=vmem,
         scratch_shapes=[
+            pltpu.VMEM((count, width), bf16),
             pltpu.VMEM((width, unit), bf16),
             pltpu.VMEM((width, unit), bf16),
             pltpu.VMEM((unit, width), bf16),
@@ -261,14 +297,16 @@
             pltpu.VMEM((n, ROWS, piece + LANES), bf16),
             pltpu.VMEM((n * ROWS, unit), f32),
             pltpu.VMEM((n * ROWS, unit), f32),
-            pltpu.VMEM((chips, 2, half, block), bf16),
+            pltpu.VMEM((chips, half, block), f32),
+            pltpu.VMEM((chips, half, block), bf16),
             pltpu.VMEM((chips, half, block), bf16),
             pltpu.VMEM((chips, half, block), bf16),
             pltpu.VMEM((chips, half, block), bf16),
             pltpu.VMEM((chips, count, rank), f32),
             pltpu.VMEM((chips, count, rank), f32),
+            dma((4,)),
             dma((3,)),
-            dma((2,)),
+            dma((chips,)),
             dma((chips,)),
             dma((chips,)),
             dma((n,)),
@@ -280,9 +318,9 @@
             dma((chips,)),
         ],
         compiler_params=pltpu.CompilerParams(
-            collective_id=0, has_side_effects=True, vmem_limit_bytes=40 * 2**20
+            collective_id=0, has_side_effects=True, vmem_limit_bytes=60 * 2**20
         ),
-    )(tokens, expert_ids, gate_codes, gate_weight, up_weight, down_weight, target_basis)
+    )(tokens, expert_ids.T, gate_codes.T, gate_weight, up_weight, down_weight, target_basis)
 
 
 def shards(tokens, expert_ids, gate_codes, gate_weight, up_weight, down_weight, target_basis):

time: 55.4 us -> 40.8 us (0.74)
  local copies, waits for them, and re-layouts: 10.1 us -> 1.28 us
  Pallas kernels: 45 us -> 39.3 us
    unnamed x13 -> x1, local copies, waits for them, and re-layouts: 10.1 us -> 1.28 us
    pallas_call x1, Pallas kernels: 45 us -> 39.3 us  [fused(): pl.pallas_call(functools.partial(kernel, n), out_shape=jax.ShapeDtypeStru...]
where the time goes in v2:
time: 40.8 us; the launch traced here: 40.6 us
  Pallas kernels  39.3 us (96%)
  local copies, waits for them, and re-layouts  1.28 us (3%)
    pallas_call x1, Pallas kernels, fused(): pl.pallas_call(functools.partial(kernel, n), out_shape=jax.ShapeDtypeStru...  39.3 us
    unnamed x1, local copies, waits for them, and re-layouts  1.28 us

profile of v2, /device:TPU:0, one launch (start us, length us, event | category | flops | bytes accessed | tf_op | source)
XLA Modules:
  0.0 40.6 jit_solution(2647218548548232796)
XLA Ops:
  0.0 39.3 %shard_map.73 = bf16[4,512]{1,0:T(4,128)(2,1)} custom-call(bf16[4,7168]{1,0:T(4,128)(2,1)} %tok_in.1, s32[2,4]{1,0:T(2,128)} %bitcast.2, s32[2,4]{1,0:T(2,128)} %bitcast.3, bf16[1,7168,256]{2,1,0:T(8,128)(2,1)} %gw.1, bf16[1,7168,256]{2,1,0:T(8,128)(2,1)} %uw.1, bf16[1,256,7168]{2,1,0:T(8,128)(2,1)} %dw.1, bf16[448,512]{1,0:T(8,128)(2,1)} %basis.1), custom_call_target="tpu_custom_call" | custom-call | tf_op jit(solution)/shard_map/pallas_call | solution.py:286
  39.3 1.3 %copy.9 = bf16[4,512]{1,0:T(4,128)(2,1)} copy(bf16[4,512]{1,0:T(4,128)(2,1)} %shard_map.73) | data formatting | bytes 8192

commit v3 on v2

--- a/solution.py
+++ b/solution.py
@@ -64,8 +64,8 @@
 
 def kernel(
     n, tok_in, ids, codes, gw, uw, dw, basis, out,
-    tok, wg, wu, wd, bs, x, accg, accu, yown, ypart, yexch, yout, yrecv, zsend, zrecv,
-    w_sem, b_sem, own_send, side_send, fwd_send, x_recv, e_send, e_recv, y_send, y_recv, z_send, z_recv,
+    tok, wg, wu, wd, bs, x, accg, accu, yown, ypart, yexch, yout, yside, yrecv, zsend, zrecv,
+    w_sem, b_sem, own_send, side_send, fwd_send, x_recv, e_send, e_recv, y_send, s_recv, y_recv, z_send, z_recv,
 ):
     f32, bf16 = jnp.float32, jnp.bfloat16
     count, width = tok.shape
@@ -213,11 +213,12 @@
     )
 
     loads[2].wait()
-    z = None
+    order = steps + [0]
+    turns = [(k, d) for d in range(across - 1, -1, -1) for k in order]
     lag = 2
-    for k in range(chips + lag):
-        if k < chips:
-            to = (chip + 1 + k) % chips
+    for t in range(chips + lag):
+        if t < chips:
+            to = at(a + turns[t][0], b + turns[t][1], 0) // 2
             y = jnp.dot(
                 hidden,
                 wd[:, pl.ds(pl.multiple_of(to * block, LANES), block)],
@@ -229,21 +230,37 @@
             c.start()
             sends.append(c)
             yown[to] = y[:half]
-        if k >= lag:
-            to = (chip + 1 + k - lag) % chips
+        if t >= lag:
+            k, d = turns[t - lag]
+            to = at(a + k, b + d, 0) // 2
             remote(yexch.at[to], yexch.at[to], e_send.at[to], e_recv.at[to], sib).wait_recv()
             summed = yown[to] + yexch[to].astype(f32)
-            if k - lag == chips - 1:
-                z = summed
+            if d == 0:
+                yown[to] = summed
             else:
                 yout[to] = summed.astype(bf16)
+                slot = (a + k) % along
                 c = remote(
-                    yout.at[to], yrecv.at[chip], y_send.at[to], y_recv.at[chip], to * 2 + core
+                    yout.at[to], yside.at[slot], y_send.at[to], s_recv.at[slot], at(a, b + 1, core)
                 )
                 c.start()
                 sends.append(c)
-    for k in range(1, chips):
-        src = (chip + chips - k) % chips
+    for k in order:
+        slot = (a + k) % along
+        to = at(a + k, b, 0) // 2
+        z = yown[to]
+        if across == 2:
+            remote(
+                yside.at[slot], yside.at[slot], y_send.at[to], s_recv.at[slot], sib
+            ).wait_recv()
+            z = z + yside[slot].astype(f32)
+        if k:
+            yout[to] = z.astype(bf16)
+            c = remote(yout.at[to], yrecv.at[a], y_send.at[to], y_recv.at[a], at(a + k, b, core))
+            c.start()
+            sends.append(c)
+    for k in steps:
+        src = (a + along - k) % along
         remote(yrecv.at[src], yrecv.at[src], y_send.at[src], y_recv.at[src], sib).wait_recv()
         z = z + yrecv[src].astype(f32)
 
@@ -302,6 +319,7 @@
             pltpu.VMEM((chips, half, block), bf16),
             pltpu.VMEM((chips, half, block), bf16),
             pltpu.VMEM((chips, half, block), bf16),
+            pltpu.VMEM((chips, half, block), bf16),
             pltpu.VMEM((chips, count, rank), f32),
             pltpu.VMEM((chips, count, rank), f32),
             dma((4,)),
@@ -310,6 +328,7 @@
             dma((chips,)),
             dma((chips,)),
             dma((n,)),
+            dma((chips,)),
             dma((chips,)),
             dma((chips,)),
             dma((chips,)),

time: 40.8 us -> 39.2 us (0.961)
  Pallas kernels: 39.3 us -> 37.7 us
    pallas_call x1, Pallas kernels: 39.3 us -> 37.7 us  [fused(): pl.pallas_call(functools.partial(kernel, n), out_shape=jax.ShapeDtypeStru...]
where the time goes in v3:
time: 39.2 us; the launch traced here: 39 us
  Pallas kernels  37.7 us (96%)
  local copies, waits for them, and re-layouts  1.28 us (3%)
    pallas_call x1, Pallas kernels, fused(): pl.pallas_call(functools.partial(kernel, n), out_shape=jax.ShapeDtypeStru...  37.7 us
    unnamed x1, local copies, waits for them, and re-layouts  1.28 us

profile of v3, /device:TPU:0, one launch (start us, length us, event | category | flops | bytes accessed | tf_op | source)
XLA Modules:
  0.0 39.0 jit_solution(9782936008785469697)
XLA Ops:
  0.0 37.7 %shard_map.73 = bf16[4,512]{1,0:T(4,128)(2,1)} custom-call(bf16[4,7168]{1,0:T(4,128)(2,1)} %tok_in.1, s32[2,4]{1,0:T(2,128)} %bitcast.2, s32[2,4]{1,0:T(2,128)} %bitcast.3, bf16[1,7168,256]{2,1,0:T(8,128)(2,1)} %gw.1, bf16[1,7168,256]{2,1,0:T(8,128)(2,1)} %uw.1, bf16[1,256,7168]{2,1,0:T(8,128)(2,1)} %dw.1, bf16[448,512]{1,0:T(8,128)(2,1)} %basis.1), custom_call_target="tpu_custom_call" | custom-call | tf_op jit(solution)/shard_map/pallas_call | solution.py:303
  37.7 1.3 %copy.9 = bf16[4,512]{1,0:T(4,128)(2,1)} copy(bf16[4,512]{1,0:T(4,128)(2,1)} %shard_map.73) | data formatting | bytes 8192

commit v4 on v3

--- a/solution.py
+++ b/solution.py
@@ -86,6 +86,10 @@
         return (a % along * across + b % across) * 2 + c
 
 
+    def place_of(dev):
+        owner = dev // 2
+        return (owner % across * along + owner // across) * 2 + dev % 2
+
     def remote(src, dst, ssem, rsem, dev):
         return pltpu.make_async_remote_copy(
             src_ref=src, dst_ref=dst, send_sem=ssem, recv_sem=rsem,
@@ -136,18 +140,30 @@
         ],
         axis=0,
     )
-    x[me] = own.astype(bf16)
+    x[place_of(me)] = own.astype(bf16)
     pl.semaphore_wait(barrier, chips)
 
     sends = []
 
     def pass_on(src, sem, dev):
-        c = remote(x.at[src], x.at[src], sem, x_recv.at[src], dev)
+        slot = place_of(src)
+        c = remote(x.at[slot], x.at[slot], sem, x_recv.at[slot], dev)
         c.start()
         sends.append(c)
 
     def arrived(src):
-        remote(x.at[src], x.at[src], own_send.at[0], x_recv.at[src], sib).wait_recv()
+        slot = place_of(src)
+        remote(x.at[slot], x.at[slot], own_send.at[0], x_recv.at[slot], sib).wait_recv()
+
+    lines = along * 2 * ROWS
+    place = lax.broadcasted_iota(jnp.int32, (lines, 1), 0) % ROWS // count
+
+    def part(q, col):
+        left = x[pl.ds(col * (along * 2), along * 2), :, 0:piece].reshape(lines, piece)
+        to = pl.ds(pl.multiple_of(col * lines, ROWS), lines)
+        for w, acc in ((wg, accg), (wu, accu)):
+            v = jnp.dot(left, w[q * piece : (q + 1) * piece, :], preferred_element_type=f32)
+            acc[to, :] = v if q == 0 else jnp.where(place == q, v, acc[to, :])
 
     steps = [k for k in (1, along - 1) if 0 < k < along]
     steps = list(dict.fromkeys(steps + list(range(1, along))))
@@ -162,33 +178,26 @@
         if across == 2:
             pass_on(src, side_send.at[k], at(a, b + 1, core))
         pass_on(src, fwd_send.at[k], sib)
+    cb = remote(basis, bs.at[core], b_sem.at[0], b_sem.at[1], sib)
+    cb.start()
+    for k in [0] + steps:
+        arrived(at(a + along - k, b, 1 - core))
+    loads[0].wait()
+    loads[1].wait()
+    others = [at(a + along - k, b + 1, core) for k in [0] + steps] if across == 2 else []
+    for q in range(max(parts, len(others))):
+        if q < parts:
+            part(q, b)
+        if q < len(others):
+            arrived(others[q])
+            pass_on(others[q], fwd_send.at[along + q], sib)
     if across == 2:
         for k in [0] + steps:
-            src = at(a + along - k, b + 1, core)
-            arrived(src)
-            pass_on(src, fwd_send.at[along + k], sib)
-    cb = remote(basis, bs.at[core], b_sem.at[0], b_sem.at[1], sib)
-    cb.start()
-    for k in range(chips):
-        arrived(((chip + k) % chips) * 2 + 1 - core)
-    loads[0].wait()
-    loads[1].wait()
+            arrived(at(a + along - k, b + 1, 1 - core))
+        for q in range(parts):
+            part(q, 1 - b)
 
     total = n * ROWS
-    place = lax.broadcasted_iota(jnp.int32, (total, 1), 0) % ROWS // count
-    left = x[:, :, 0:piece].reshape(total, piece)
-
-    def part(q, carry):
-        span = pl.ds(pl.multiple_of(q * piece, LANES), piece)
-        g = jnp.dot(left, wg[span, :], preferred_element_type=f32)
-        accg[...] = jnp.where(place == q, g, accg[...])
-        u = jnp.dot(left, wu[span, :], preferred_element_type=f32)
-        accu[...] = jnp.where(place == q, u, accu[...])
-        return carry
-
-    accg[...] = jnp.zeros_like(accg)
-    accu[...] = jnp.zeros_like(accu)
-    lax.fori_loop(0, parts, part, 0)
 
     def fold(v):
         step = count
@@ -202,7 +211,7 @@
     i = lax.broadcasted_iota(jnp.int32, (n * count, total), 0)
     owner = i % half // count * 2 + (i // half + core) % 2
     j = lax.broadcasted_iota(jnp.int32, (n * count, total), 1)
-    pick = jnp.where(j == owner * ROWS + i % count, 1.0, 0.0).astype(bf16)
+    pick = jnp.where(j == place_of(owner) * ROWS + i % count, 1.0, 0.0).astype(bf16)
     hidden = jnp.dot(pick, hidden, preferred_element_type=f32).astype(bf16)
     tail = x[:, :, piece:].reshape(total, LANES)
     tail = jnp.dot(pick, tail, preferred_element_type=f32)

time: 39.2 us -> 37.5 us (0.957)
  Pallas kernels: 37.7 us -> 36.1 us
    pallas_call x1, Pallas kernels: 37.7 us -> 36.1 us  [fused(): pl.pallas_call(functools.partial(kernel, n), out_shape=jax.ShapeDtypeStru...]
where the time goes in v4:
time: 37.5 us; the launch traced here: 37.3 us
  Pallas kernels  36.1 us (96%)
  local copies, waits for them, and re-layouts  1.28 us (3%)
    pallas_call x1, Pallas kernels, fused(): pl.pallas_call(functools.partial(kernel, n), out_shape=jax.ShapeDtypeStru...  36.1 us
    unnamed x1, local copies, waits for them, and re-layouts  1.28 us

profile of v4, /device:TPU:0, one launch (start us, length us, event | category | flops | bytes accessed | tf_op | source)
XLA Modules:
  0.0 37.3 jit_solution(12679364481122486004)
XLA Ops:
  0.0 36.1 %shard_map.73 = bf16[4,512]{1,0:T(4,128)(2,1)} custom-call(bf16[4,7168]{1,0:T(4,128)(2,1)} %tok_in.1, s32[2,4]{1,0:T(2,128)} %bitcast.2, s32[2,4]{1,0:T(2,128)} %bitcast.3, bf16[1,7168,256]{2,1,0:T(8,128)(2,1)} %gw.1, bf16[1,7168,256]{2,1,0:T(8,128)(2,1)} %uw.1, bf16[1,256,7168]{2,1,0:T(8,128)(2,1)} %dw.1, bf16[448,512]{1,0:T(8,128)(2,1)} %basis.1), custom_call_target="tpu_custom_call" | custom-call | tf_op jit(solution)/shard_map/pallas_call | solution.py:312
  36.1 1.3 %copy.9 = bf16[4,512]{1,0:T(4,128)(2,1)} copy(bf16[4,512]{1,0:T(4,128)(2,1)} %shard_map.73) | data formatting | bytes 8192
